TPU v7x, 128 devices: a whole 4x4x4 slice. The times are simulated.
128 devices in a mesh: store: 4 (over z), req: 32 (over x, y, core).
Axes of the slice: x: 4, y: 4, z: 4, core: 2. Of those that a mesh axis runs over, the one named last changes fastest.
Arguments:
- hidden: bfloat16 [20480, 8192], P('req', 'store'), may hold values from -6 to 6
- norm_gain: float32 [8192], replicated, may hold values from 0.1 to 1.9
- w_query: bfloat16 [8192, 4096], P(None, 'store'), may hold values from -0.0625 to 0.0625
- w_key: bfloat16 [8192, 512], P(None, 'store'), may hold values from -0.0625 to 0.0625
- w_value: bfloat16 [8192, 512], P(None, 'store'), may hold values from -0.0625 to 0.0625
- passage_cache: bfloat16 [256, 4, 256, 256], P('req', 'store'), may hold values from -6 to 6
- sys_cache: bfloat16 [1024, 4, 256], P('req', 'store'), may hold values from -800 to 800
- passage_place: int32 [256], replicated, may hold values from 0 to 255, as said below
- passage_ids: int32 [256, 4], P('req'), may hold values from 0 to 255, as said below
- passage_count: int32 [256], P('req'), may hold values from 3 to 4
- recompute_pos: int32 [256, 80], P('req'), may hold values from 0 to 1023, as said below
Outputs:
- attended: bfloat16 [20480, 4096], P('req', 'store')
Inputs may be any that keep to these rules, and one draw needn't show every extreme that they name: `passage_place`: A permutation of the storage positions. `passage_ids`: slot j of request r is valid when j < passage_count[r]; padded slots hold ids too. Over the requests of one index of req, at most 2 valid slots name passages whose storage position lies on one index of req (passage_place // 8); ids may repeat. `recompute_pos`: distinct and rising along each row; entries at or past passage_count * 256 of their request are padding.
All inputs are finite; a program needn't handle non-finite values.
Results may differ from a plain program's by a relative error of at most 0.023.
The roundings to bfloat16 on the way count: a program that leaves them out, or rounds other values in their place, can miss the bound.
Values may be sent and summed in bfloat16 or wider, within the bound.
A program may use at most 192 MiB of HBM per device.

v0:
```python
import jax
import jax.numpy as jnp
from jax import lax
from jax.sharding import PartitionSpec as P

HD = 128
GROUP = 8
PT = 256
MAXP = 4
RT = 80


def body(
    hidden,
    norm_gain,
    w_query,
    w_key,
    w_value,
    passage_cache,
    sys_cache,
    passage_place,
    passage_ids,
    passage_count,
    recompute_pos,
):
    local_reqs = passage_ids.shape[0]
    token_rows = local_reqs * RT
    kv_local = w_key.shape[1] // HD
    full = lax.all_gather(hidden, "store", axis=1, tiled=True)
    widened = full.astype(jnp.float32)
    inverse_rms = lax.rsqrt(jnp.mean(widened * widened, axis=1, keepdims=True) + 1e-05)
    normed = (widened * inverse_rms * norm_gain).astype(jnp.bfloat16)
    queries = jnp.dot(normed, w_query, preferred_element_type=jnp.float32).astype(jnp.bfloat16)
    queries = queries.reshape(local_reqs, RT, kv_local, GROUP, HD)
    keys_new = jnp.dot(normed, w_key, preferred_element_type=jnp.float32).astype(jnp.bfloat16)
    values_new = jnp.dot(normed, w_value, preferred_element_type=jnp.float32).astype(jnp.bfloat16)
    fresh = jnp.concatenate(
        [
            keys_new.reshape(local_reqs, RT, kv_local, HD),
            values_new.reshape(local_reqs, RT, kv_local, HD),
        ],
        axis=3,
    )
    fresh = fresh.transpose(0, 2, 1, 3)
    prompt = lax.all_gather(sys_cache, "req", axis=0, tiled=True).transpose(1, 0, 2)
    prompt_rows = prompt.shape[1]
    slots = local_reqs * MAXP
    span = passage_cache.shape[1] * passage_cache.shape[2] * passage_cache.shape[3]
    spots_flat = passage_place[passage_ids].reshape(slots)
    piece = lax.all_gather(passage_cache, "req", axis=0, tiled=True)
    piece_rows = piece.shape[0]
    selector = (spots_flat[:, None] == jnp.arange(piece_rows, dtype=jnp.int32)[None, :]).astype(
        jnp.bfloat16
    )
    gathered = jnp.dot(
        selector, piece.reshape(piece_rows, span), preferred_element_type=jnp.float32
    )
    fetched = gathered.astype(jnp.bfloat16)
    context = fetched.reshape(local_reqs, MAXP, kv_local, PT, 2 * HD).transpose(0, 2, 1, 3, 4)
    context = context.reshape(local_reqs, kv_local, MAXP * PT, 2 * HD)
    offsets = jnp.arange(MAXP * PT, dtype=jnp.int32)
    scale = HD ** (-0.5)

    def one_request(items):
        block_context, valid_count, positions, query_block, fresh_block = items
        hot = positions[:, None] == offsets[None, :]
        placed = jnp.einsum(
            "rt,krd->ktd", hot.astype(jnp.bfloat16), fresh_block, preferred_element_type=jnp.float32
        ).astype(jnp.bfloat16)
        touched = jnp.any(hot, axis=0)
        block_context = jnp.where(touched[None, :, None], placed, block_context)
        keyvals = jnp.concatenate([prompt, block_context], axis=1)
        scores = (
            jnp.einsum(
                "rkgd,knd->kgrn",
                query_block,
                keyvals[:, :, :HD],
                preferred_element_type=jnp.float32,
            )
            * scale
        )
        allowed = (offsets[None, :] <= positions[:, None]) & (offsets[None, :] < valid_count * PT)
        allowed = jnp.concatenate([jnp.ones((RT, prompt_rows), dtype=bool), allowed], axis=1)
        scores = jnp.where(allowed[None, None], scores, -1e30)
        largest = jnp.max(scores, axis=3, keepdims=True)
        weights = jnp.exp(scores - largest)
        total = jnp.sum(weights, axis=3, keepdims=True)
        mixed = jnp.einsum(
            "kgrn,knd->kgrd",
            weights.astype(jnp.bfloat16),
            keyvals[:, :, HD:],
            preferred_element_type=jnp.float32,
        )
        result = (mixed / total).astype(jnp.bfloat16)
        return result.transpose(2, 0, 1, 3).reshape(RT, kv_local * GROUP * HD)

    attended = lax.map(one_request, (context, passage_count, recompute_pos, queries, fresh))
    return attended.reshape(token_rows, kv_local * GROUP * HD)


def solution(mesh):
    placed = (
        P("req", "store"),
        P(),
        P(None, "store"),
        P(None, "store"),
        P(None, "store"),
        P("req", "store", None, None),
        P("req", "store", None),
        P(),
        P("req", None),
        P("req"),
        P("req", None),
    )
    return jax.shard_map(
        body, mesh=mesh, in_specs=placed, out_specs=P("req", "store"), check_vma=False
    )
```

profile of v0, /device:TPU:1, one launch (start us, length us, event | category | flops | bytes accessed | tf_op | source)
XLA Modules:
  0.0 369.7 jit_solution(11341591413457126591)
XLA Ops:
  8.9 26.4 %all_gather.11 = bf16[1024,1,256]{2,0,1:T(8,128)(2,1)S(1)} all-gather(bf16[32,1,256]{2,0,1:T(8,128)(2,1)} %param.19), channel_id=1, replica_groups=mesh['store'=4,'req'=32] {'req'}, dimensions={0}, use_global_device_ids=true | all-gather | bytes 540672 | tf_op jit(solution)/shard_map/all_gather | solution.py:45
  35.3 1.0 copy.30
  37.0 76.1 %all-gather.3.cloned.1.call-done = bf16[640,8192]{1,0:T(8,128)(2,1)} async-done(((bf16[640,2048]{1,0:T(8,128)(2,1)}), bf16[640,8192]{1,0:T(8,128)(2,1)}) %all-gather.3.cloned.1.call-update) | async-done | bytes 10485776 | tf_op jit(solution)/shard_map/all_gather | solution.py:29
  113.2 6.2 %fusion.38 = f32[640]{0:T(1024)S(1)} fusion(bf16[640,8192]{1,0:T(8,128)(2,1)} %all-gather.3.cloned.1.call-done), kind=kLoop, calls=%fused_computation.46 | loop fusion | flops 15728000 | bytes 10488320 | tf_op jit(solution)/shard_map/reduce_sum | solution.py:31
  120.1 15.7 %fusion.41 = bf16[80,8,8,128]{3,1,2,0:T(8,128)(2,1)} fusion(bf16[8192,1024]{1,0:T(8,128)(2,1)} %param.15, bf16[640,8192]{1,0:T(8,128)(2,1)S(1)} %copy-done.3, f32[8192]{0:T(1024)S(1)} %copy-done.6, f32[640]{0:T(1024)S(1)} %add_rsqrt_fusion), kind=kOutput, calls=%fused_computation.50 | convolution fusion | flops 10759045120 | bytes 28609024 | tf_op jit(solution)/shard_map/dot_general | solution.py:33
  135.8 2.8 copy.39
  138.6 2.9 convolution_convert_fusion.4
  141.5 3.0 convolution_convert_fusion.3
  144.5 86.0 %all-gather.5.cloned.1.call-done = bf16[256,1,256,256]{3,2,1,0:T(8,128)(2,1)} async-done(((bf16[8,1,256,256]{3,2,1,0:T(8,128)(2,1)}), bf16[256,1,256,256]{3,2,1,0:T(8,128)(2,1)}) %all-gather.5.cloned.1.call-update) | async-done | bytes 33554448 | tf_op jit(solution)/shard_map/all_gather | solution.py:50
  230.6 31.0 %copy.38 = bf16[32,8,256,256]{3,1,2,0:T(8,128)(2,1)} copy(bf16[32,8,256,256]{3,2,1,0:T(8,128)(2,1)} %bitcast.112) | data formatting | bytes 67108864
  261.6 18.3 %convolution_convert_fusion.1 = bf16[32,65536]{1,0:T(8,128)(2,1)} fusion(bf16[256,65536]{1,0:T(8,128)(2,1)} %bitcast.111, s32[32]{0:T(128)S(1)} %gather_fusion), kind=kOutput, calls=%fused_computation.43 | convolution fusion | flops 1075847168 | bytes 37748864 | tf_op jit(solution)/shard_map/dot_general | solution.py:55
  279.9 5.7 %reshape_transpose_reshape.3 = bf16[8,1,1024,256]{3,2,0,1:T(8,128)(2,1)} reshape(bf16[32,65536]{1,0:T(8,128)(2,1)} %convolution_convert_fusion.1) | data formatting | bytes 8388608 | tf_op jit(solution)/shard_map/reshape;transpose;reshape | solution.py:60
  285.6 75.7 %while.12 = (s32[]{:T(128)}, bf16[8,80,1024]{2,1,0:T(8,128)(2,1)}, s32[8,80]{1,0:T(8,128)}, s32[8]{0:T(128)S(1)}, bf16[8,1,80,256]{3,2,1,0:T(8,128)(2,1)S(1)}, /...) while((s32[]{:T(128)}, bf16[8,80,1024]{2,1,0:T(8,128)(2,1)}, ...), condition=%wide.region_5.6_spmd.clone.clone, body=%wide.region_1.5_spmd.clone.clone.sunk | while | flops 730643200 | bytes 23489112 | solution.py:97
  287.8 1.1 constant_dynamic-slice_fusion.6
  289.5 0.9 constant_dynamic-slice_fusion.5
  290.5 1.1 fusion.65
  291.6 1.3 fusion.66
  292.9 1.3 fusion.67
  297.3 1.1 constant_dynamic-slice_fusion.6
  299.0 0.9 constant_dynamic-slice_fusion.5
  299.9 1.1 fusion.65
  301.0 1.3 fusion.66
  302.3 1.3 fusion.67
  306.7 1.1 constant_dynamic-slice_fusion.6
  309.4 1.1 fusion.65
  310.5 1.3 fusion.66
  311.8 1.3 fusion.67
  316.2 1.1 constant_dynamic-slice_fusion.6
  318.8 1.1 fusion.65
  319.9 1.3 fusion.66
  321.3 1.3 fusion.67
  325.6 1.1 constant_dynamic-slice_fusion.6
  328.3 1.1 fusion.65
  329.4 1.3 fusion.66
  330.7 1.3 fusion.67
  335.1 1.1 constant_dynamic-slice_fusion.6
  337.7 1.1 fusion.65
  338.8 1.3 fusion.66
  340.2 1.3 fusion.67
  344.6 1.1 constant_dynamic-slice_fusion.6
  347.2 1.1 fusion.65
  348.3 1.3 fusion.66
  349.6 1.3 fusion.67
  354.0 1.1 constant_dynamic-slice_fusion.6
  356.7 1.1 fusion.65
  357.8 1.3 fusion.66
  359.1 1.3 fusion.67
  361.2 1.6 copy-done.1
  (113 shorter events, 32.9 us)
Async XLA Ops:
  6.5 132.0 %copy-start = (bf16[8192,128]{1,0:T(8,128)(2,1)S(1)}, bf16[8192,128]{1,0:T(8,128)(2,1)}, u32[]{:S(2)}) copy-start(bf16[8192,128]{1,0:T(8,128)(2,1)} %param.16) | copy-start | bytes 6291460
  6.5 29.8 %copy-start.2 = (s32[256]{0:T(256)S(1)}, s32[256]{0:T(256)}, u32[]{:S(2)}) copy-start(s32[256]{0:T(256)} %param.20) | copy-start | bytes 3076
  6.5 106.6 %all-gather.3.cloned.1.call-start = ((), (), s32[]{:S(2)}) async-start(), calls=%async_computation | async-start | bytes 13107200 | tf_op jit(solution)/shard_map/all_gather | solution.py:29
  7.3 223.3 %all-gather.5.cloned.1.call-start = ((), (), s32[]{:S(2)}) async-start(), calls=%async_computation.1 | async-start | bytes 34603008 | tf_op jit(solution)/shard_map/all_gather | solution.py:50
  36.3 83.1 %copy-start.6 = (f32[8192]{0:T(1024)S(1)}, f32[8192]{0:T(1024)}, u32[]{:S(2)}) copy-start(f32[8192]{0:T(1024)} %param.14) | copy-start | bytes 98308
  113.2 7.0 %copy-start.3 = (bf16[640,8192]{1,0:T(8,128)(2,1)S(1)}, bf16[640,8192]{1,0:T(8,128)(2,1)}, u32[]{:S(2)}) copy-start(bf16[640,8192]{1,0:T(8,128)(2,1)} %all-gather.3.cloned.1.call-done) | copy-start | bytes 31457284
  138.6 2.9 copy-start.5
  279.9 5.7 %copy-start.4 = (bf16[1,1024,256]{1,2,0:T(8,128)(2,1)S(1)}, bf16[1,1024,256]{1,2,0:T(8,128)(2,1)}, u32[]{:S(2)}) copy-start(bf16[1,1024,256]{1,2,0:T(8,128)(2,1)} %copy.30) | copy-start | bytes 1572868
  279.9 5.7 %copy-start.7 = (s32[8]{0:T(128)S(1)}, s32[8]{0:T(128)}, u32[]{:S(2)}) copy-start(s32[8]{0:T(128)} %param.22) | copy-start | bytes 100
  361.2 1.6 copy-start.1
Sparse Core Ops, SparseCore 0:
  9.0 104.0 all-gather.2
  115.4 115.1 all-gather.4
where the time goes:
time: 371 us; the launch traced here: 370 us
  waiting for transfers between devices  164 us (44%)
  local copies, waits for them, and re-layouts  79 us (21%)
  matrix products  62.1 us (17%)
  blocking collectives  26.4 us (7%)
  other arithmetic  19 us (5%)
  between operations  13.5 us (4%)
  loops' own time  6.08 us (2%)
    all_gather x1, waiting for transfers between devices, body(): piece = lax.all_gather(passage_cache, 'req', axis=0, tiled=True)  86 us
    all_gather x1, waiting for transfers between devices, body(): full = lax.all_gather(hidden, 'store', axis=1, tiled=True)  76.1 us
    unnamed x19, local copies, waits for them, and re-layouts  37.1 us
    all_gather x1, blocking collectives, body(): lax.all_gather(sys_cache, 'req', axis=0, tiled=True).transpose(1, 0, 2)  26.4 us
    dynamic_slice x32, local copies, waits for them, and re-layouts, body(): lax.map(one_request, (context, passage_count, recompute_pos, queries, fre...  23.1 us
    dot_general x1, matrix products, body(): jnp.dot(selector, piece.reshape(piece_rows, span), preferred_element_type...  18.3 us
    dot_general x1, matrix products, body(): jnp.dot(normed, w_query, preferred_element_type=jnp.float32)  15.7 us
    reduce_sum x8, other arithmetic, one_request(): total = jnp.sum(weights, axis=3, keepdims=True)  10.6 us
  transfers between devices with their start and end apart: 2, of which 2 were waited for; matrix products, arithmetic and copies ran while one was open for 9% of the time, Pallas kernels for 0%

commit v1 on v0

v1 whole, which is shorter than its diff:
```python
import jax
import jax.numpy as jnp
from jax import lax
from jax.experimental import pallas as pl
from jax.experimental.pallas import tpu as pltpu
from jax.sharding import PartitionSpec as P

HD = 128
GROUP = 8
PT = 256
MAXP = 4
RT = 80
SIDE = 4
FEAT = 2048
REQ_DEV = 8
STORED = 8
CAP = 2
SLOTS = SIDE * CAP
SYS = 1024
SYS_DEV = 32
WT = 256
ROWS = GROUP * RT
HALF = ROWS // 2
FAR = 1 << 20
LOW = -1e30
EXP_SCALE = HD ** (-0.5) * 1.4426950408889634
MESH = pl.DeviceIdType.MESH


def kernel(
    hidden,
    gain,
    w_query,
    w_key,
    w_value,
    stored,
    sys_own,
    wish,
    spot,
    code,
    limit,
    out,
    weights,
    tokens,
    normed,
    along,
    along_sys,
    picked,
    held,
    held_sys,
    wishes,
    wishes_s,
    projected,
    part_mix,
    part_stat,
    z_send,
    z_recv,
    a_send,
    a_recv,
    as_send,
    as_recv,
    w_send,
    w_recv,
    b_send,
    b_recv,
    bs_send,
    bs_recv,
    local,
):
    z = lax.axis_index("store")
    req = lax.axis_index("req")
    x = req // 8
    y = lax.rem(req // 2, 4)
    c = lax.rem(req, 2)
    a_pos = x * (1 - c) + y * c
    b_pos = y * (1 - c) + x * c

    def at(xx, yy, cc):
        return (z, (lax.rem(xx, 4) * 4 + lax.rem(yy, 4)) * 2 + cc)

    def along_dev(d):
        return at(x + d * (1 - c), y + d * c, c)

    def asker(db, dc):
        cc = c if dc == 0 else 1 - c
        return at(x + db * c, y + db * (1 - c), cc)

    def via(e, dc):
        cc = c if dc == 0 else 1 - c
        return at(x + e * cc, y + e * (1 - cc), cc)

    def via_index(e, dc):
        cc = c if dc == 0 else 1 - c
        return cc * 4 + lax.rem(y * (1 - cc) + x * cc + e, 4)

    right = (lax.rem(z + 1, 4), req)
    left = (lax.rem(z + 3, 4), req)
    me_via = c * 4 + b_pos

    pieces = []
    for j in range(4):
        pieces.append((w_query.at[:, pl.ds(j * WT, WT)], weights.at[j]))
    pieces.append((w_key, weights.at[4, :, pl.ds(0, HD)]))
    pieces.append((w_value, weights.at[4, :, pl.ds(HD, HD)]))
    pieces.append((hidden, tokens.at[0]))
    pieces.append((stored, along.at[a_pos]))
    pieces.append((sys_own, along_sys.at[a_pos]))
    pieces.append((wish, wishes.at[0]))
    loads = [pltpu.make_async_copy(s, d, local.at[i]) for i, (s, d) in enumerate(pieces)]

    barrier = pltpu.get_barrier_semaphore()
    partners = [left, right, at(x, y, 1 - c)]
    for d in range(1, 4):
        for cc in range(2):
            partners.append(at(x + d, y, cc))
            partners.append(at(x, y + d, cc))
    for device in partners:
        pl.semaphore_signal(barrier, inc=1, device_id=device, device_id_type=MESH)
    for load in loads:
        load.start()
    pl.semaphore_wait(barrier, len(partners))

    def remote(src, dst, send, recv, device):
        return pltpu.make_async_remote_copy(
            src_ref=src,
            dst_ref=dst,
            send_sem=send,
            recv_sem=recv,
            device_id=device,
            device_id_type=MESH,
        )

    def rows_of(t):
        return pl.ds(pl.multiple_of(t * RT, 16), RT)

    def z_own(t, way):
        return remote(
            hidden.at[rows_of(t)],
            tokens.at[1 + way, rows_of(t)],
            z_send.at[way, t],
            z_recv.at[way, t],
            (right, left)[way],
        )

    def z_pass(t, way):
        cols = pl.ds(way * (FEAT // 2), FEAT // 2)
        return remote(
            tokens.at[1 + way, rows_of(t), cols],
            tokens.at[3, rows_of(t), cols],
            z_send.at[2 + way, t],
            z_recv.at[2 + way, t],
            (right, left)[way],
        )

    def a_copy(d, pos):
        return remote(stored, along.at[pos], a_send.at[d - 1], a_recv.at[d - 1], along_dev(d))

    def as_copy(d, pos):
        return remote(sys_own, along_sys.at[pos], as_send.at[d - 1], as_recv.at[d - 1], along_dev(d))

    def wish_copy(e, dc):
        slot = ((4 - e) % 4) * 2 + dc
        return remote(wish, wishes.at[slot], w_send.at[slot], w_recv.at[slot], via(e, dc))

    def b_copy(db, dc, index):
        q = db * 2 + dc
        return remote(picked.at[q], held.at[index], b_send.at[q], b_recv.at[q], asker(db, dc))

    def bs_copy(db, dc, index):
        q = db * 2 + dc
        return remote(along_sys, held_sys.at[index], bs_send.at[q], bs_recv.at[q], asker(db, dc))

    others = [(db, dc) for db in (1, 3, 2, 0) for dc in range(2) if (db, dc) != (0, 0)]

    for way in range(2):
        z_own(0, way).start()
    for db, dc in others:
        wish_copy((4 - db) % 4, dc).start()
    for d in (1, 3, 2):
        as_copy(d, a_pos).start()
    for d in (1, 3, 2):
        a_copy(d, a_pos).start()
    for way in range(2):
        z_own(1, way).start()
    for load in loads:
        load.wait()

    def fetch():
        for db, dc in others:
            wish_copy((4 - db) % 4, dc).wait_recv()
        copy = pltpu.make_async_copy(wishes, wishes_s, local.at[0])
        copy.start()
        for d in (1, 3, 2):
            as_copy(d, lax.rem(a_pos + 4 - d, 4)).wait_recv()
        for db, dc in others:
            bs_copy(db, dc, me_via).start()
        held_sys[me_via] = along_sys[...]
        copy.wait()
        for d in (1, 3, 2):
            a_copy(d, lax.rem(a_pos + 4 - d, 4)).wait_recv()
        for db, dc in others:
            q = db * 2 + dc

            def pick(k, _, q=q):
                row = wishes_s[q, me_via, k]
                picked[q, k] = along[k // CAP, row]
                return 0

            lax.fori_loop(0, SLOTS, pick, 0)
            b_copy(db, dc, me_via).start()

        def keep(k, _):
            row = wishes_s[0, me_via, k]
            held[me_via, k] = along[k // CAP, row]
            return 0

        lax.fori_loop(0, SLOTS, keep, 0)

    spread = (0, 3, 1, 2)

    def project(k):
        for step in range(2):
            for way in range(2):
                z_pass(2 * k + step, way).wait_recv()

        def norm(i, _):
            rows = pl.ds(pl.multiple_of(k * (2 * RT) + i * 16, 16), 16)
            total = jnp.zeros((16, 1), jnp.float32)
            for slot in range(4):
                wide = tokens[slot, rows, :].astype(jnp.float32)
                total = total + jnp.sum(wide * wide, axis=1, keepdims=True)
            inverse = lax.rsqrt(total * (1.0 / (4 * FEAT)) + 1e-05)
            to = pl.ds(pl.multiple_of(i * 16, 16), 16)
            for slot in range(4):
                source = lax.rem(z + spread[slot], 4)
                cols = pl.ds(pl.multiple_of(source * FEAT, FEAT), FEAT)
                wide = tokens[slot, rows, :].astype(jnp.float32)
                normed[source, to, :] = (wide * inverse * gain[:, cols]).astype(jnp.bfloat16)
            return 0

        lax.fori_loop(0, 2 * RT // 16, norm, 0)

        def tile(j, _):
            total = jnp.zeros((2 * RT, WT), jnp.float32)
            for source in range(4):
                total = total + jnp.dot(
                    normed[source],
                    weights[j, pl.ds(source * FEAT, FEAT), :],
                    preferred_element_type=jnp.float32,
                )
            low = total.astype(jnp.bfloat16)
            for half in range(2):
                for step in range(2):
                    to = pl.ds(pl.multiple_of((2 * j + half) * RT, 16), RT)
                    projected[2 * k + step, to, :] = low[
                        step * RT : (step + 1) * RT, half * HD : (half + 1) * HD
                    ]
            return 0

        lax.fori_loop(0, 5, tile, 0)

    def dot_t(a, b):
        return lax.dot_general(a, b, (((1,), (1,)), ((), ())), preferred_element_type=jnp.float32)

    def half_rows(hb):
        return pl.ds(pl.multiple_of(hb * HALF, 16), HALF)

    def shared(i, _):
        r = i // 2
        rows = half_rows(lax.rem(i, 2))
        query = projected[r, rows, :]
        keyvals = held_sys[...].reshape(SYS, 2 * HD)
        scores = dot_t(query, keyvals[:, :HD])
        largest = jnp.max(scores, axis=1, keepdims=True)
        part = jnp.exp2((scores - largest) * EXP_SCALE)
        total = jnp.sum(part, axis=1, keepdims=True)
        mix = jnp.dot(
            part.astype(jnp.bfloat16), keyvals[:, HD:], preferred_element_type=jnp.float32
        )
        slot = lax.rem(r, 4)
        part_mix[slot, rows, :] = mix
        lane = lax.broadcasted_iota(jnp.int32, (HALF, HD), 1)
        part_stat[slot, rows, :] = jnp.where(lane < HD // 2, largest, total)
        return 0

    def own(i, _):
        r = i // 2
        hb = lax.rem(i, 2)
        rows = half_rows(hb)
        slot = lax.rem(r, 4)
        query = projected[r, rows, :]
        allowed_to = jnp.concatenate([limit[r]] * (GROUP // 2), axis=0)
        codes = code[r]
        spots = [spot[r * MAXP + j] for j in range(MAXP)]
        scores = []
        for j in range(MAXP):
            keys = held[spots[j] // SLOTS, lax.rem(spots[j], SLOTS), :, pl.ds(0, HD)]
            allowed = codes[:, j * PT : (j + 1) * PT] <= allowed_to
            scores.append(jnp.where(allowed, dot_t(query, keys), LOW))
        keys = projected[r, pl.ds(ROWS, RT), :]
        allowed = codes[:, MAXP * PT : MAXP * PT + RT] <= allowed_to
        scores.append(jnp.where(allowed, dot_t(query, keys), LOW))
        stat = part_stat[slot, rows, :]
        sys_largest = stat[:, 0:1]
        sys_total = stat[:, HD // 2 : HD // 2 + 1]
        largest = sys_largest
        for one in scores:
            largest = jnp.maximum(largest, jnp.max(one, axis=1, keepdims=True))
        shrink = jnp.exp2((sys_largest - largest) * EXP_SCALE)
        total = sys_total * shrink
        mix = part_mix[slot, rows, :] * shrink
        for j in range(MAXP + 1):
            part = jnp.exp2((scores[j] - largest) * EXP_SCALE)
            total = total + jnp.sum(part, axis=1, keepdims=True)
            if j < MAXP:
                values = held[spots[j] // SLOTS, lax.rem(spots[j], SLOTS), :, pl.ds(HD, HD)]
            else:
                values = projected[r, pl.ds(ROWS + RT, RT), :]
            mix = mix + jnp.dot(
                part.astype(jnp.bfloat16), values, preferred_element_type=jnp.float32
            )
        result = (mix / total).astype(jnp.bfloat16)
        to = pl.ds(pl.multiple_of(r * RT, 16), RT)
        for h in range(GROUP // 2):
            cols = pl.ds(pl.multiple_of((hb * (GROUP // 2) + h) * HD, HD), HD)
            out[to, cols] = result[h * RT : (h + 1) * RT, :]
        return 0

    def step(t, _):
        @pl.when(t < 8)
        def _():
            for way in range(2):
                z_own(t, way).wait_recv()
                z_pass(t, way).start()

            @pl.when(t < 6)
            def _():
                for way in range(2):
                    z_own(t + 2, way).start()

        @pl.when(t == 1)
        def _():
            fetch()

        @pl.when(t == 3)
        def _():
            for db, dc in others:
                bs_copy(db, dc, via_index((4 - db) % 4, dc)).wait_recv()

        @pl.when((t == 3) | (t == 5) | (t >= 7))
        def _():
            k = (t - 2) // 2
            project(k)
            lax.fori_loop(4 * k, 4 * k + 4, shared, 0)

        @pl.when(t == 6)
        def _():
            for db, dc in others:
                b_copy(db, dc, via_index((4 - db) % 4, dc)).wait_recv()

        @pl.when(t >= 6)
        def _():
            begin = jnp.where(t == 6, 0, 4 * t - 20)
            end = 4 * t - 16
            lax.fori_loop(begin, end, own, 0)

        return 0

    lax.fori_loop(0, 9, step, 0)

    def finish(t, _):
        for way in range(2):
            z_own(t, way).wait_send()
            z_pass(t, way).wait_send()
        return 0

    lax.fori_loop(0, 8, finish, 0)
    for d in (1, 3, 2):
        a_copy(d, a_pos).wait_send()
        as_copy(d, a_pos).wait_send()
    for db, dc in others:
        wish_copy((4 - db) % 4, dc).wait_send()
        b_copy(db, dc, me_via).wait_send()
        bs_copy(db, dc, me_via).wait_send()


def tables(passage_place, passage_ids, passage_count, recompute_pos):
    slots = REQ_DEV * MAXP
    place = passage_place[passage_ids.reshape(slots)]
    valid = (jnp.arange(MAXP)[None, :] < passage_count[:, None]).reshape(slots)
    holder = place // STORED
    row = lax.rem(place, STORED)
    xs, ys, cs = holder // 8, lax.rem(holder // 2, 4), lax.rem(holder, 2)
    order = jnp.arange(slots)
    before = (order[None, :] < order[:, None]) & (holder[None, :] == holder[:, None]) & valid[None, :]
    rank = jnp.minimum(jnp.sum(before.astype(jnp.int32), axis=1), CAP - 1)
    through = cs * 4 + jnp.where(cs == 0, ys, xs)
    index = through * SLOTS + jnp.where(cs == 0, xs, ys) * CAP + rank
    cells = jnp.arange(8 * 128).reshape(8, 128)
    cell = through * 128 + lax.rem(index, SLOTS)
    wish = jnp.sum(
        jnp.where((cells[:, :, None] == cell[None, None, :]) & valid[None, None, :], row, 0), axis=2
    ).astype(jnp.int32)
    table = index.reshape(REQ_DEV, MAXP)
    spot = jnp.where(valid.reshape(REQ_DEV, MAXP), table, table[:, :1]).reshape(slots)
    span = MAXP * PT
    offsets = jnp.arange(span, dtype=jnp.int32)
    touched = jnp.any(recompute_pos[:, :, None] == offsets[None, None, :], axis=1)
    code = jnp.where(touched, FAR, offsets[None, :])
    code = jnp.concatenate(
        [code, recompute_pos, jnp.full((REQ_DEV, 128 - RT), FAR, jnp.int32)], axis=1
    )
    limit = jnp.minimum(recompute_pos, passage_count[:, None] * PT - 1)
    return (
        wish,
        spot.astype(jnp.int32),
        code.reshape(REQ_DEV, 1, span + 128).astype(jnp.int32),
        limit.reshape(REQ_DEV, RT, 1).astype(jnp.int32),
    )


def body(
    hidden,
    norm_gain,
    w_query,
    w_key,
    w_value,
    passage_cache,
    sys_cache,
    passage_place,
    passage_ids,
    passage_count,
    recompute_pos,
):
    wish, spot, code, limit = tables(passage_place, passage_ids, passage_count, recompute_pos)
    anywhere = pl.BlockSpec(memory_space=pl.ANY)
    vmem = pl.BlockSpec(memory_space=pltpu.VMEM)
    smem = pl.BlockSpec(memory_space=pltpu.SMEM)
    bf16 = jnp.bfloat16
    dma = pltpu.SemaphoreType.DMA
    return pl.pallas_call(
        kernel,
        out_shape=jax.ShapeDtypeStruct((REQ_DEV * RT, GROUP * HD), bf16),
        in_specs=[
            anywhere,
            vmem,
            anywhere,
            anywhere,
            anywhere,
            anywhere,
            vmem,
            vmem,
            smem,
            vmem,
            vmem,
        ],
        out_specs=vmem,
        scratch_shapes=[
            pltpu.VMEM((5, 4 * FEAT, WT), bf16),
            pltpu.VMEM((4, REQ_DEV * RT, FEAT), bf16),
            pltpu.VMEM((4, 2 * RT, FEAT), bf16),
            pltpu.VMEM((SIDE, STORED, PT, 2 * HD), bf16),
            pltpu.VMEM((SIDE, SYS_DEV, 2 * HD), bf16),
            pltpu.VMEM((8, SLOTS, PT, 2 * HD), bf16),
            pltpu.VMEM((8, SLOTS, PT, 2 * HD), bf16),
            pltpu.VMEM((8, SIDE, SYS_DEV, 2 * HD), bf16),
            pltpu.VMEM((8, 8, 128), jnp.int32),
            pltpu.SMEM((8, 8, 128), jnp.int32),
            pltpu.VMEM((REQ_DEV, 10 * RT, HD), bf16),
            pltpu.VMEM((4, ROWS, HD), jnp.float32),
            pltpu.VMEM((4, ROWS, HD), jnp.float32),
            dma((4, 8)),
            dma((4, 8)),
            dma((3,)),
            dma((3,)),
            dma((3,)),
            dma((3,)),
            dma((8,)),
            dma((8,)),
            dma((8,)),
            dma((8,)),
            dma((8,)),
            dma((8,)),
            dma((10,)),
        ],
        compiler_params=pltpu.CompilerParams(
            collective_id=0, has_side_effects=True, vmem_limit_bytes=64 * 1024 * 1024
        ),
    )(
        hidden,
        norm_gain.reshape(1, 4 * FEAT),
        w_query,
        w_key,
        w_value,
        passage_cache.reshape(STORED, PT, 2 * HD),
        sys_cache.reshape(SYS_DEV, 2 * HD),
        wish,
        spot,
        code,
        limit,
    )


def solution(mesh):
    placed = (
        P("req", "store"),
        P(),
        P(None, "store"),
        P(None, "store"),
        P(None, "store"),
        P("req", "store", None, None),
        P("req", "store", None),
        P(),
        P("req", None),
        P("req"),
        P("req", None),
    )
    return jax.shard_map(
        body, mesh=mesh, in_specs=placed, out_specs=P("req", "store"), check_vma=False
    )
```

time: 371 us -> 140 us (0.38)
  waiting for transfers between devices: 164 us -> 0 us
  Pallas kernels: 0 us -> 127 us
  local copies, waits for them, and re-layouts: 79 us -> 7.5 us
  matrix products: 62.1 us -> 0 us
  blocking collectives: 26.4 us -> 0 us
  other arithmetic: 19 us -> 5.07 us
  between operations: 13.5 us -> 0.06 us
  loops' own time: 6.08 us -> 0 us
    all_gather x2 -> x0, waiting for transfers between devices: 162 us -> none  [the longest x1 86 us: body(): piece = lax.all_gather(passage_cache, 'req', axis=0, tiled=True)]
    pallas_call x0 -> x1, Pallas kernels: none -> 127 us  [body(): pl.pallas_call(kernel, out_shape=jax.ShapeDtypeStruct((REQ_DEV * RT, GROU...]
    dot_general x28 -> x0, matrix products: 62.1 us -> none  [the longest x1 18.3 us: body(): jnp.dot(selector, piece.reshape(piece_rows, span), preferred_element_type...]
    unnamed x19 -> x2, local copies, waits for them, and re-layouts: 37.1 us -> 3.22 us
    all_gather x1 -> x0, blocking collectives: 26.4 us -> none  [body(): lax.all_gather(sys_cache, 'req', axis=0, tiled=True).transpose(1, 0, 2)]
    dynamic_slice x32 -> x0, local copies, waits for them, and re-layouts: 23.1 us -> none  [body(): lax.map(one_request, (context, passage_count, recompute_pos, queries, fre...]
    reduce_sum x9 -> x2, other arithmetic: 16.9 us -> 0.88 us  [the longest x1 0.7 us: tables(): jnp.sum(jnp.where((cells[:, :, None] == cell[None, None, :]) & valid[None...]
    another operation x1 -> x0, loops' own time: 6.08 us -> none  [body(): lax.map(one_request, (context, passage_count, recompute_pos, queries, fre...]
  transfers between devices with their start and end apart: 2 -> 0, of which waited for: 2 -> 0; matrix products, arithmetic and copies ran while one was open for 9% -> 0% of each run, Pallas kernels for 0% -> 0%
where the time goes in v1:
time: 140 us
  Pallas kernels  127 us (91%)
  local copies, waits for them, and re-layouts  7.5 us (5%)
  other arithmetic  5.07 us (4%)
    pallas_call x1, Pallas kernels, body(): pl.pallas_call(kernel, out_shape=jax.ShapeDtypeStruct((REQ_DEV * RT, GROU...  127 us
    unnamed x2, local copies, waits for them, and re-layouts  3.22 us

profile of v1, /device:TPU:1, one launch (start us, length us, event | category | flops | bytes accessed | tf_op | source)
XLA Modules:
  0.0 139.7 jit_solution(14120597559744629243)
XLA Ops:
  0.0 0.7 multiply_add_fusion.1
  0.7 0.7 iota_compare_fusion.2
  1.4 0.1 lt.55
  1.5 0.8 minimum_bitcast_fusion
  2.2 0.8 copy.15
  3.0 0.1 reshape.202
  3.1 1.4 gather_fusion
  4.5 0.2 convert_reduce_fusion
  4.7 0.1 min.22
  4.8 0.1 gather.6
  4.9 0.1 slice_reduce_fusion
  5.0 0.1 broadcast_in_dim.50
  5.1 0.1 broadcast_in_dim.51
  5.2 0.6 fusion.18
  5.7 0.7 select_reduce_fusion.wish
  6.4 1.4 fusion
  7.9 0.8 concatenate.3
  8.6 0.6 reshape.203.code
  9.3 0.9 copy.16.limit
  10.2 127.1 %shard_map.109 = bf16[640,1024]{1,0:T(8,128)(2,1)} custom-call(bf16[640,2048]{1,0:T(8,128)(2,1)} %hidden.1, f32[1,8192]{1,0:T(1,128)} %bitcast.8, bf16[8192,1024]{1,0:T(8,128)(2,1)} %w_query.1, bf16[8192,128]{1,0:T(8,128)(2,1)} %w_key.1, bf16[8192,128]{1,0:T(8,128)(2,1)} %w_value.1, bf16[8,256,256]{2,1,0:T(8,128)(2,1)} %bitcast.7, bf16[32,256]{1,0:T(8,128)(2,1)} %bitcast.9, ...), custom_call_target="tpu_custom_call" | custom-call | tf_op jit(solution)/shard_map/pallas_call | solution.py:441
  137.3 2.5 %copy.18 = bf16[640,1024]{1,0:T(8,128)(2,1)} copy(bf16[640,1024]{1,0:T(8,128)(2,1)} %shard_map.109) | data formatting | bytes 2621440
  (9 shorter events, 0.1 us)

commit v2 on v1

--- a/solution.py
+++ b/solution.py
@@ -35,21 +35,30 @@
     w_value,
     stored,
     sys_own,
-    wish,
-    spot,
-    code,
-    limit,
+    place,
+    ids,
+    count,
+    pos,
     out,
     weights,
     tokens,
     normed,
-    along,
+    along_own,
+    along_one,
+    along_two,
+    along_three,
     along_sys,
     picked,
     held,
     held_sys,
+    mine,
+    mine_s,
     wishes,
     wishes_s,
+    holder_s,
+    spot,
+    code,
+    limit,
     projected,
     part_mix,
     part_stat,
@@ -96,6 +105,7 @@
     right = (lax.rem(z + 1, 4), req)
     left = (lax.rem(z + 3, 4), req)
     me_via = c * 4 + b_pos
+    along = (along_own, along_one, along_two, along_three)
 
     pieces = []
     for j in range(4):
@@ -103,9 +113,8 @@
     pieces.append((w_key, weights.at[4, :, pl.ds(0, HD)]))
     pieces.append((w_value, weights.at[4, :, pl.ds(HD, HD)]))
     pieces.append((hidden, tokens.at[0]))
-    pieces.append((stored, along.at[a_pos]))
+    pieces.append((stored, along_own))
     pieces.append((sys_own, along_sys.at[a_pos]))
-    pieces.append((wish, wishes.at[0]))
     loads = [pltpu.make_async_copy(s, d, local.at[i]) for i, (s, d) in enumerate(pieces)]
 
     barrier = pltpu.get_barrier_semaphore()
@@ -152,19 +161,32 @@
             (right, left)[way],
         )
 
-    def a_copy(d, pos):
-        return remote(stored, along.at[pos], a_send.at[d - 1], a_recv.at[d - 1], along_dev(d))
-
-    def as_copy(d, pos):
-        return remote(sys_own, along_sys.at[pos], as_send.at[d - 1], as_recv.at[d - 1], along_dev(d))
+    def a_copy(d):
+        return remote(stored, along[d], a_send.at[d - 1], a_recv.at[d - 1], along_dev(d))
+
+    def a_pass(d):
+        part = pl.ds(0 if d == 1 else STORED // 2, STORED // 2)
+        return remote(
+            along[d].at[part], along_two.at[part], a_send.at[d], a_recv.at[d], along_dev(d)
+        )
+
+    def as_copy(d, at_pos):
+        return remote(sys_own, along_sys.at[at_pos], as_send.at[d - 1], as_recv.at[d - 1], along_dev(d))
 
     def wish_copy(e, dc):
         slot = ((4 - e) % 4) * 2 + dc
-        return remote(wish, wishes.at[slot], w_send.at[slot], w_recv.at[slot], via(e, dc))
-
-    def b_copy(db, dc, index):
+        return remote(mine, wishes.at[slot - 1], w_send.at[slot], w_recv.at[slot], via(e, dc))
+
+    def b_copy(db, dc, off, index):
         q = db * 2 + dc
-        return remote(picked.at[q], held.at[index], b_send.at[q], b_recv.at[q], asker(db, dc))
+        part = pl.ds(off * CAP, CAP)
+        return remote(
+            picked.at[q, part],
+            held.at[index, part],
+            b_send.at[q, off],
+            b_recv.at[q, off],
+            asker(db, dc),
+        )
 
     def bs_copy(db, dc, index):
         q = db * 2 + dc
@@ -174,47 +196,100 @@
 
     for way in range(2):
         z_own(0, way).start()
+    for d in (1, 3, 2):
+        as_copy(d, a_pos).start()
+    for d in (1, 3):
+        a_copy(d).start()
+    for way in range(2):
+        z_own(1, way).start()
+
+    cells = lax.broadcasted_iota(jnp.int32, (8, 128), 0) * 128 + lax.broadcasted_iota(
+        jnp.int32, (8, 128), 1
+    )
+
+    def ask(i, wish):
+        r = i // MAXP
+        stands = place[ids[lax.rem(i, MAXP), r]]
+        valid = lax.rem(i, MAXP) < count[r]
+        holder = lax.div(stands, STORED)
+        row = lax.rem(stands, STORED)
+        hx, hy, hc = lax.div(holder, 8), lax.rem(lax.div(holder, 2), 4), lax.rem(holder, 2)
+        rank = 0
+        for j in range(REQ_DEV * MAXP):
+            rank = rank + jnp.where(holder_s[j] == holder, 1, 0)
+        rank = jnp.minimum(rank, CAP - 1)
+        holder_s[i] = jnp.where(valid, holder, -1)
+        through = hc * 4 + hy * (1 - hc) + hx * hc
+        ahead = (hx - x + 4) * (1 - hc) + (hy - y + 4) * hc
+        which = lax.rem(ahead, 4) * CAP + rank
+        spot[i] = jnp.where(valid, through * SLOTS + which, spot[r * MAXP])
+        cell = jnp.where(valid, through * 128 + which, -1)
+        return jnp.where(cells == cell, row, wish)
+
+    for i in range(REQ_DEV * MAXP):
+        holder_s[i] = -1
+        spot[i] = 0
+    mine[...] = lax.fori_loop(0, REQ_DEV * MAXP, ask, jnp.zeros((8, 128), jnp.int32))
     for db, dc in others:
         wish_copy((4 - db) % 4, dc).start()
-    for d in (1, 3, 2):
-        as_copy(d, a_pos).start()
-    for d in (1, 3, 2):
-        a_copy(d, a_pos).start()
-    for way in range(2):
-        z_own(1, way).start()
-    for load in loads:
-        load.wait()
-
-    def fetch():
-        for db, dc in others:
-            wish_copy((4 - db) % 4, dc).wait_recv()
-        copy = pltpu.make_async_copy(wishes, wishes_s, local.at[0])
-        copy.start()
+
+    def mark(r, _):
+        line = pos[pl.ds(r, 1), :]
+        wide = jnp.broadcast_to(line, (RT, RT))
+        eye = lax.broadcasted_iota(jnp.int32, (RT, RT), 0) == lax.broadcasted_iota(
+            jnp.int32, (RT, RT), 1
+        )
+        column = jnp.sum(jnp.where(eye, wide, 0), axis=1, keepdims=True)
+        limit[r] = jnp.minimum(column, count[r] * PT - 1)
+        offsets = lax.broadcasted_iota(jnp.int32, (RT, MAXP * PT), 1)
+        touched = jnp.max(jnp.where(offsets == column, FAR, 0), axis=0, keepdims=True)
+        code[r, :, pl.ds(0, MAXP * PT)] = jnp.maximum(touched, offsets[0:1, :])
+        code[r, :, pl.ds(MAXP * PT, RT)] = line
+        return 0
+
+    lax.fori_loop(0, REQ_DEV, mark, 0)
+
+    def give(off):
+        rows = along[(4 - off) % 4]
+        for db, dc in others + [(0, 0)]:
+            q = db * 2 + dc
+            for rank in range(CAP):
+                k = off * CAP + rank
+                row = wishes_s[q - 1, me_via, k] if q else mine_s[me_via, k]
+                if q:
+                    picked[q, k] = rows[row]
+                else:
+                    held[me_via, k] = rows[row]
+            if q:
+                b_copy(db, dc, off, me_via).start()
+
+    def give_own():
+        for load in loads:
+            load.wait()
         for d in (1, 3, 2):
             as_copy(d, lax.rem(a_pos + 4 - d, 4)).wait_recv()
         for db, dc in others:
             bs_copy(db, dc, me_via).start()
         held_sys[me_via] = along_sys[...]
-        copy.wait()
-        for d in (1, 3, 2):
-            a_copy(d, lax.rem(a_pos + 4 - d, 4)).wait_recv()
         for db, dc in others:
-            q = db * 2 + dc
-
-            def pick(k, _, q=q):
-                row = wishes_s[q, me_via, k]
-                picked[q, k] = along[k // CAP, row]
-                return 0
-
-            lax.fori_loop(0, SLOTS, pick, 0)
-            b_copy(db, dc, me_via).start()
-
-        def keep(k, _):
-            row = wishes_s[0, me_via, k]
-            held[me_via, k] = along[k // CAP, row]
-            return 0
-
-        lax.fori_loop(0, SLOTS, keep, 0)
+            wish_copy((4 - db) % 4, dc).wait_recv()
+        for source, target in ((wishes, wishes_s), (mine, mine_s)):
+            copy = pltpu.make_async_copy(source, target, local.at[0])
+            copy.start()
+            copy.wait()
+        give(0)
+
+    def give_near():
+        for d in (1, 3):
+            a_copy(d).wait_recv()
+            a_pass(d).start()
+        give(3)
+        give(1)
+
+    def give_far():
+        for d in (1, 3):
+            a_pass(d).wait_recv()
+        give(2)
 
     spread = (0, 3, 1, 2)
 
@@ -338,9 +413,17 @@
                 for way in range(2):
                     z_own(t + 2, way).start()
 
+        @pl.when(t == 0)
+        def _():
+            give_own()
+
         @pl.when(t == 1)
         def _():
-            fetch()
+            give_near()
+
+        @pl.when(t == 2)
+        def _():
+            give_far()
 
         @pl.when(t == 3)
         def _():
@@ -356,7 +439,8 @@
         @pl.when(t == 6)
         def _():
             for db, dc in others:
-                b_copy(db, dc, via_index((4 - db) % 4, dc)).wait_recv()
+                for off in range(SIDE):
+                    b_copy(db, dc, off, via_index((4 - db) % 4, dc)).wait_recv()
 
         @pl.when(t >= 6)
         def _():
@@ -375,48 +459,16 @@
         return 0
 
     lax.fori_loop(0, 8, finish, 0)
+    for d in (1, 3):
+        a_copy(d).wait_send()
+        a_pass(d).wait_send()
     for d in (1, 3, 2):
-        a_copy(d, a_pos).wait_send()
         as_copy(d, a_pos).wait_send()
     for db, dc in others:
         wish_copy((4 - db) % 4, dc).wait_send()
-        b_copy(db, dc, me_via).wait_send()
+        for off in range(SIDE):
+            b_copy(db, dc, off, me_via).wait_send()
         bs_copy(db, dc, me_via).wait_send()
-
-
-def tables(passage_place, passage_ids, passage_count, recompute_pos):
-    slots = REQ_DEV * MAXP
-    place = passage_place[passage_ids.reshape(slots)]
-    valid = (jnp.arange(MAXP)[None, :] < passage_count[:, None]).reshape(slots)
-    holder = place // STORED
-    row = lax.rem(place, STORED)
-    xs, ys, cs = holder // 8, lax.rem(holder // 2, 4), lax.rem(holder, 2)
-    order = jnp.arange(slots)
-    before = (order[None, :] < order[:, None]) & (holder[None, :] == holder[:, None]) & valid[None, :]
-    rank = jnp.minimum(jnp.sum(before.astype(jnp.int32), axis=1), CAP - 1)
-    through = cs * 4 + jnp.where(cs == 0, ys, xs)
-    index = through * SLOTS + jnp.where(cs == 0, xs, ys) * CAP + rank
-    cells = jnp.arange(8 * 128).reshape(8, 128)
-    cell = through * 128 + lax.rem(index, SLOTS)
-    wish = jnp.sum(
-        jnp.where((cells[:, :, None] == cell[None, None, :]) & valid[None, None, :], row, 0), axis=2
-    ).astype(jnp.int32)
-    table = index.reshape(REQ_DEV, MAXP)
-    spot = jnp.where(valid.reshape(REQ_DEV, MAXP), table, table[:, :1]).reshape(slots)
-    span = MAXP * PT
-    offsets = jnp.arange(span, dtype=jnp.int32)
-    touched = jnp.any(recompute_pos[:, :, None] == offsets[None, None, :], axis=1)
-    code = jnp.where(touched, FAR, offsets[None, :])
-    code = jnp.concatenate(
-        [code, recompute_pos, jnp.full((REQ_DEV, 128 - RT), FAR, jnp.int32)], axis=1
-    )
-    limit = jnp.minimum(recompute_pos, passage_count[:, None] * PT - 1)
-    return (
-        wish,
-        spot.astype(jnp.int32),
-        code.reshape(REQ_DEV, 1, span + 128).astype(jnp.int32),
-        limit.reshape(REQ_DEV, RT, 1).astype(jnp.int32),
-    )
 
 
 def body(
@@ -432,7 +484,6 @@
     passage_count,
     recompute_pos,
 ):
-    wish, spot, code, limit = tables(passage_place, passage_ids, passage_count, recompute_pos)
     anywhere = pl.BlockSpec(memory_space=pl.ANY)
     vmem = pl.BlockSpec(memory_space=pltpu.VMEM)
     smem = pl.BlockSpec(memory_space=pltpu.SMEM)
@@ -449,9 +500,9 @@
             anywhere,
             anywhere,
             vmem,
-            vmem,
             smem,
-            vmem,
+            smem,
+            smem,
             vmem,
         ],
         out_specs=vmem,
@@ -459,29 +510,38 @@
             pltpu.VMEM((5, 4 * FEAT, WT), bf16),
             pltpu.VMEM((4, REQ_DEV * RT, FEAT), bf16),
             pltpu.VMEM((4, 2 * RT, FEAT), bf16),
-            pltpu.VMEM((SIDE, STORED, PT, 2 * HD), bf16),
+            pltpu.VMEM((STORED, PT, 2 * HD), bf16),
+            pltpu.VMEM((STORED, PT, 2 * HD), bf16),
+            pltpu.VMEM((STORED, PT, 2 * HD), bf16),
+            pltpu.VMEM((STORED, PT, 2 * HD), bf16),
             pltpu.VMEM((SIDE, SYS_DEV, 2 * HD), bf16),
             pltpu.VMEM((8, SLOTS, PT, 2 * HD), bf16),
             pltpu.VMEM((8, SLOTS, PT, 2 * HD), bf16),
             pltpu.VMEM((8, SIDE, SYS_DEV, 2 * HD), bf16),
-            pltpu.VMEM((8, 8, 128), jnp.int32),
-            pltpu.SMEM((8, 8, 128), jnp.int32),
+            pltpu.VMEM((8, 128), jnp.int32),
+            pltpu.SMEM((8, 128), jnp.int32),
+            pltpu.VMEM((7, 8, 128), jnp.int32),
+            pltpu.SMEM((7, 8, 128), jnp.int32),
+            pltpu.SMEM((REQ_DEV * MAXP,), jnp.int32),
+            pltpu.SMEM((REQ_DEV * MAXP,), jnp.int32),
+            pltpu.VMEM((REQ_DEV, 1, MAXP * PT + 128), jnp.int32),
+            pltpu.VMEM((REQ_DEV, RT, 1), jnp.int32),
             pltpu.VMEM((REQ_DEV, 10 * RT, HD), bf16),
             pltpu.VMEM((4, ROWS, HD), jnp.float32),
             pltpu.VMEM((4, ROWS, HD), jnp.float32),
             dma((4, 8)),
             dma((4, 8)),
-            dma((3,)),
-            dma((3,)),
+            dma((4,)),
+            dma((4,)),
             dma((3,)),
             dma((3,)),
             dma((8,)),
             dma((8,)),
+            dma((8, SIDE)),
+            dma((8, SIDE)),
             dma((8,)),
             dma((8,)),
-            dma((8,)),
-            dma((8,)),
-            dma((10,)),
+            dma((9,)),
         ],
         compiler_params=pltpu.CompilerParams(
             collective_id=0, has_side_effects=True, vmem_limit_bytes=64 * 1024 * 1024
@@ -494,10 +554,10 @@
         w_value,
         passage_cache.reshape(STORED, PT, 2 * HD),
         sys_cache.reshape(SYS_DEV, 2 * HD),
-        wish,
-        spot,
-        code,
-        limit,
+        passage_place,
+        passage_ids.T,
+        passage_count,
+        recompute_pos,
     )
 
 

time: 140 us -> 123 us (0.88)
  Pallas kernels: 127 us -> 120 us
  other arithmetic: 5.07 us -> 0 us
  local copies, waits for them, and re-layouts: 7.5 us -> 2.47 us
    pallas_call x1, Pallas kernels: 127 us -> 120 us  [body(): pl.pallas_call(kernel, out_shape=jax.ShapeDtypeStruct((REQ_DEV * RT, GROU...]
    reshape x3 -> x0, local copies, waits for them, and re-layouts: 1.61 us -> none  [the longest x1 0.9 us: tables(): limit.reshape(REQ_DEV, RT, 1).astype(jnp.int32)]
    gather x2 -> x0, local copies, waits for them, and re-layouts: 1.47 us -> none  [tables(): place = passage_place[passage_ids.reshape(slots)]]
    unnamed x2 -> x1, local copies, waits for them, and re-layouts: 3.22 us -> 2.47 us
where the time goes in v2:
time: 123 us; the launch traced here: 122 us
  Pallas kernels  120 us (98%)
  local copies, waits for them, and re-layouts  2.47 us (2%)
    pallas_call x1, Pallas kernels, body(): pl.pallas_call(kernel, out_shape=jax.ShapeDtypeStruct((REQ_DEV * RT, GROU...  120 us
    unnamed x1, local copies, waits for them, and re-layouts  2.47 us

profile of v2, /device:TPU:1, one launch (start us, length us, event | category | flops | bytes accessed | tf_op | source)
XLA Modules:
  0.0 122.4 jit_solution(1635497846955167650)
XLA Ops:
  0.0 119.9 %shard_map.109 = bf16[640,1024]{1,0:T(8,128)(2,1)} custom-call(bf16[640,2048]{1,0:T(8,128)(2,1)} %hidden.1, f32[1,8192]{1,0:T(1,128)} %bitcast.5, bf16[8192,1024]{1,0:T(8,128)(2,1)} %w_query.1, bf16[8192,128]{1,0:T(8,128)(2,1)} %w_key.1, bf16[8192,128]{1,0:T(8,128)(2,1)} %w_value.1, bf16[8,256,256]{2,1,0:T(8,128)(2,1)} %bitcast.4, bf16[32,256]{1,0:T(8,128)(2,1)} %bitcast.6, ...), custom_call_target="tpu_custom_call" | custom-call | tf_op jit(solution)/shard_map/pallas_call | solution.py:492
  119.9 2.5 %copy.13 = bf16[640,1024]{1,0:T(8,128)(2,1)} copy(bf16[640,1024]{1,0:T(8,128)(2,1)} %shard_map.109) | data formatting | bytes 2621440

commit v3 on v2

--- a/solution.py
+++ b/solution.py
@@ -57,13 +57,18 @@
     wishes_s,
     holder_s,
     spot,
-    code,
-    limit,
     projected,
     part_mix,
     part_stat,
+    partial,
+    square_own,
+    square_in,
+    inverse,
+    bias,
     z_send,
     z_recv,
+    q_send,
+    q_recv,
     a_send,
     a_recv,
     as_send,
@@ -118,14 +123,15 @@
     loads = [pltpu.make_async_copy(s, d, local.at[i]) for i, (s, d) in enumerate(pieces)]
 
     barrier = pltpu.get_barrier_semaphore()
-    partners = [left, right, at(x, y, 1 - c)]
+    opposite = (lax.rem(z + 2, 4), req)
+    partners = [left, right, opposite, at(x, y, 1 - c)]
     for d in range(1, 4):
         for cc in range(2):
             partners.append(at(x + d, y, cc))
             partners.append(at(x, y + d, cc))
     for device in partners:
         pl.semaphore_signal(barrier, inc=1, device_id=device, device_id_type=MESH)
-    for load in loads:
+    for load in loads[-3:]:
         load.start()
     pl.semaphore_wait(barrier, len(partners))
 
@@ -233,21 +239,50 @@
     for db, dc in others:
         wish_copy((4 - db) % 4, dc).start()
 
-    def mark(r, _):
+    eye = lax.broadcasted_iota(jnp.int32, (RT, RT), 0) == lax.broadcasted_iota(
+        jnp.int32, (RT, RT), 1
+    )
+
+    def square_copy(d):
+        device = (right, opposite, left)[d - 1]
+        return remote(square_own, square_in.at[d - 1], q_send.at[d - 1], q_recv.at[d - 1], device)
+
+    def square(t, _):
+        column = jnp.zeros((RT, 1), jnp.float32)
+        for part in range(FEAT // 256):
+            wide = tokens[0, rows_of(t), pl.ds(part * 256, 256)].astype(jnp.float32)
+            column = column + jnp.sum(wide * wide, axis=1, keepdims=True)
+        square_own[pl.ds(t, 1), pl.ds(0, RT)] = jnp.sum(
+            jnp.where(eye, column, 0.0), axis=0, keepdims=True
+        )
+        return 0
+
+    square_own[...] = jnp.zeros((8, 128), jnp.float32)
+    loads[-3].wait()
+    lax.fori_loop(0, 8, square, 0)
+    for d in (1, 3, 2):
+        square_copy(d).start()
+
+    def invert(t, _):
+        line = square_own[pl.ds(t, 1), pl.ds(0, RT)]
+        for d in range(3):
+            line = line + square_in[d, pl.ds(t, 1), pl.ds(0, RT)]
+        line = lax.rsqrt(line * (1.0 / (4 * FEAT)) + 1e-05)
+        inverse[rows_of(t), :] = jnp.sum(
+            jnp.where(eye, jnp.broadcast_to(line, (RT, RT)), 0.0), axis=1, keepdims=True
+        )
+        return 0
+
+    def mark(r):
         line = pos[pl.ds(r, 1), :]
         wide = jnp.broadcast_to(line, (RT, RT))
-        eye = lax.broadcasted_iota(jnp.int32, (RT, RT), 0) == lax.broadcasted_iota(
-            jnp.int32, (RT, RT), 1
-        )
         column = jnp.sum(jnp.where(eye, wide, 0), axis=1, keepdims=True)
-        limit[r] = jnp.minimum(column, count[r] * PT - 1)
+        limit = jnp.minimum(column, count[r] * PT - 1)
         offsets = lax.broadcasted_iota(jnp.int32, (RT, MAXP * PT), 1)
         touched = jnp.max(jnp.where(offsets == column, FAR, 0), axis=0, keepdims=True)
-        code[r, :, pl.ds(0, MAXP * PT)] = jnp.maximum(touched, offsets[0:1, :])
-        code[r, :, pl.ds(MAXP * PT, RT)] = line
-        return 0
-
-    lax.fori_loop(0, REQ_DEV, mark, 0)
+        stored_code = jnp.maximum(jnp.broadcast_to(touched, offsets.shape), offsets)
+        bias[:, pl.ds(0, MAXP * PT)] = jnp.where(stored_code <= limit, 0.0, LOW)
+        bias[:, pl.ds(MAXP * PT, RT)] = jnp.where(wide <= limit, 0.0, LOW)
 
     def give(off):
         rows = along[(4 - off) % 4]
@@ -264,7 +299,7 @@
                 b_copy(db, dc, off, me_via).start()
 
     def give_own():
-        for load in loads:
+        for load in loads[-2:]:
             load.wait()
         for d in (1, 3, 2):
             as_copy(d, lax.rem(a_pos + 4 - d, 4)).wait_recv()
@@ -293,37 +328,41 @@
 
     spread = (0, 3, 1, 2)
 
-    def project(k):
+    def scale(k, slots):
+        def norm(i, _):
+            rows = pl.ds(pl.multiple_of(k * (2 * RT) + i * 16, 16), 16)
+            to = pl.ds(pl.multiple_of(i * 16, 16), 16)
+            for slot in slots:
+                source = lax.rem(z + spread[slot], 4)
+                cols = pl.ds(pl.multiple_of(source * FEAT, FEAT), FEAT)
+                wide = tokens[slot, rows, :].astype(jnp.float32)
+                normed[slot, to, :] = (wide * inverse[rows, :] * gain[:, cols]).astype(jnp.bfloat16)
+            return 0
+
+        lax.fori_loop(0, 2 * RT // 16, norm, 0)
+
+    def product(j, slot):
+        source = lax.rem(z + spread[slot], 4)
+        rows = pl.ds(pl.multiple_of(source * FEAT, FEAT), FEAT)
+        return jnp.dot(normed[slot], weights[j, rows, :], preferred_element_type=jnp.float32)
+
+    def project_near(k):
+        scale(k, (0, 1, 2))
+
+        def tile(j, _):
+            partial[j] = product(j, 0) + product(j, 1) + product(j, 2)
+            return 0
+
+        lax.fori_loop(0, 5, tile, 0)
+
+    def project_far(k):
         for step in range(2):
             for way in range(2):
                 z_pass(2 * k + step, way).wait_recv()
-
-        def norm(i, _):
-            rows = pl.ds(pl.multiple_of(k * (2 * RT) + i * 16, 16), 16)
-            total = jnp.zeros((16, 1), jnp.float32)
-            for slot in range(4):
-                wide = tokens[slot, rows, :].astype(jnp.float32)
-                total = total + jnp.sum(wide * wide, axis=1, keepdims=True)
-            inverse = lax.rsqrt(total * (1.0 / (4 * FEAT)) + 1e-05)
-            to = pl.ds(pl.multiple_of(i * 16, 16), 16)
-            for slot in range(4):
-                source = lax.rem(z + spread[slot], 4)
-                cols = pl.ds(pl.multiple_of(source * FEAT, FEAT), FEAT)
-                wide = tokens[slot, rows, :].astype(jnp.float32)
-                normed[source, to, :] = (wide * inverse * gain[:, cols]).astype(jnp.bfloat16)
-            return 0
-
-        lax.fori_loop(0, 2 * RT // 16, norm, 0)
+        scale(k, (3,))
 
         def tile(j, _):
-            total = jnp.zeros((2 * RT, WT), jnp.float32)
-            for source in range(4):
-                total = total + jnp.dot(
-                    normed[source],
-                    weights[j, pl.ds(source * FEAT, FEAT), :],
-                    preferred_element_type=jnp.float32,
-                )
-            low = total.astype(jnp.bfloat16)
+            low = (partial[j] + product(j, 3)).astype(jnp.bfloat16)
             for half in range(2):
                 for step in range(2):
                     to = pl.ds(pl.multiple_of((2 * j + half) * RT, 16), RT)
@@ -338,11 +377,15 @@
         return lax.dot_general(a, b, (((1,), (1,)), ((), ())), preferred_element_type=jnp.float32)
 
     def half_rows(hb):
-        return pl.ds(pl.multiple_of(hb * HALF, 16), HALF)
-
-    def shared(i, _):
-        r = i // 2
-        rows = half_rows(lax.rem(i, 2))
+        return pl.ds(hb * HALF, HALF)
+
+    def shared(r, _):
+        for hb in range(2):
+            shared_half(r, hb)
+        return 0
+
+    def shared_half(r, hb):
+        rows = half_rows(hb)
         query = projected[r, rows, :]
         keyvals = held_sys[...].reshape(SYS, 2 * HD)
         scores = dot_t(query, keyvals[:, :HD])
@@ -352,29 +395,33 @@
         mix = jnp.dot(
             part.astype(jnp.bfloat16), keyvals[:, HD:], preferred_element_type=jnp.float32
         )
-        slot = lax.rem(r, 4)
+        slot = lax.rem(r, 6)
         part_mix[slot, rows, :] = mix
         lane = lax.broadcasted_iota(jnp.int32, (HALF, HD), 1)
         part_stat[slot, rows, :] = jnp.where(lane < HD // 2, largest, total)
+
+    def own(r, _):
+        mark(r)
+        for hb in range(2):
+            own_half(r, hb)
         return 0
 
-    def own(i, _):
-        r = i // 2
-        hb = lax.rem(i, 2)
+    def own_half(r, hb):
         rows = half_rows(hb)
-        slot = lax.rem(r, 4)
+        slot = lax.rem(r, 6)
         query = projected[r, rows, :]
-        allowed_to = jnp.concatenate([limit[r]] * (GROUP // 2), axis=0)
-        codes = code[r]
+
+        def masked(one, first, width):
+            hide = bias[:, pl.ds(first, width)]
+            return one + jnp.concatenate([hide] * (GROUP // 2), axis=0)
+
         spots = [spot[r * MAXP + j] for j in range(MAXP)]
         scores = []
         for j in range(MAXP):
             keys = held[spots[j] // SLOTS, lax.rem(spots[j], SLOTS), :, pl.ds(0, HD)]
-            allowed = codes[:, j * PT : (j + 1) * PT] <= allowed_to
-            scores.append(jnp.where(allowed, dot_t(query, keys), LOW))
+            scores.append(masked(dot_t(query, keys), j * PT, PT))
         keys = projected[r, pl.ds(ROWS, RT), :]
-        allowed = codes[:, MAXP * PT : MAXP * PT + RT] <= allowed_to
-        scores.append(jnp.where(allowed, dot_t(query, keys), LOW))
+        scores.append(masked(dot_t(query, keys), MAXP * PT, RT))
         stat = part_stat[slot, rows, :]
         sys_largest = stat[:, 0:1]
         sys_total = stat[:, HD // 2 : HD // 2 + 1]
@@ -397,9 +444,8 @@
         result = (mix / total).astype(jnp.bfloat16)
         to = pl.ds(pl.multiple_of(r * RT, 16), RT)
         for h in range(GROUP // 2):
-            cols = pl.ds(pl.multiple_of((hb * (GROUP // 2) + h) * HD, HD), HD)
+            cols = pl.ds((hb * (GROUP // 2) + h) * HD, HD)
             out[to, cols] = result[h * RT : (h + 1) * RT, :]
-        return 0
 
     def step(t, _):
         @pl.when(t < 8)
@@ -416,25 +462,40 @@
         @pl.when(t == 0)
         def _():
             give_own()
+            loads[0].start()
+            loads[1].start()
 
         @pl.when(t == 1)
         def _():
             give_near()
+            for load in loads[2:4]:
+                load.start()
 
         @pl.when(t == 2)
         def _():
             give_far()
+            for load in loads[4:-3]:
+                load.start()
+            for d in (1, 3, 2):
+                square_copy(d).wait_recv()
+            lax.fori_loop(0, 8, invert, 0)
+            for load in loads[:-3]:
+                load.wait()
 
         @pl.when(t == 3)
         def _():
             for db, dc in others:
                 bs_copy(db, dc, via_index((4 - db) % 4, dc)).wait_recv()
 
-        @pl.when((t == 3) | (t == 5) | (t >= 7))
+        @pl.when((t == 3) | (t == 4) | (t == 6) | (t == 7))
+        def _():
+            project_near(jnp.where(t > 4, t - 4, t - 3))
+
+        @pl.when((t == 3) | (t == 5) | (t == 6) | (t == 8))
         def _():
             k = (t - 2) // 2
-            project(k)
-            lax.fori_loop(4 * k, 4 * k + 4, shared, 0)
+            project_far(k)
+            lax.fori_loop(2 * k, 2 * k + 2, shared, 0)
 
         @pl.when(t == 6)
         def _():
@@ -444,8 +505,8 @@
 
         @pl.when(t >= 6)
         def _():
-            begin = jnp.where(t == 6, 0, 4 * t - 20)
-            end = 4 * t - 16
+            begin = jnp.where(t == 6, 0, 4 * t - 26)
+            end = jnp.where(t == 6, 2, 2 * t - 8)
             lax.fori_loop(begin, end, own, 0)
 
         return 0
@@ -459,6 +520,8 @@
         return 0
 
     lax.fori_loop(0, 8, finish, 0)
+    for d in (1, 3, 2):
+        square_copy(d).wait_send()
     for d in (1, 3):
         a_copy(d).wait_send()
         a_pass(d).wait_send()
@@ -524,13 +587,18 @@
             pltpu.SMEM((7, 8, 128), jnp.int32),
             pltpu.SMEM((REQ_DEV * MAXP,), jnp.int32),
             pltpu.SMEM((REQ_DEV * MAXP,), jnp.int32),
-            pltpu.VMEM((REQ_DEV, 1, MAXP * PT + 128), jnp.int32),
-            pltpu.VMEM((REQ_DEV, RT, 1), jnp.int32),
             pltpu.VMEM((REQ_DEV, 10 * RT, HD), bf16),
-            pltpu.VMEM((4, ROWS, HD), jnp.float32),
-            pltpu.VMEM((4, ROWS, HD), jnp.float32),
+            pltpu.VMEM((6, ROWS, HD), jnp.float32),
+            pltpu.VMEM((6, ROWS, HD), jnp.float32),
+            pltpu.VMEM((5, 2 * RT, WT), jnp.float32),
+            pltpu.VMEM((8, 128), jnp.float32),
+            pltpu.VMEM((3, 8, 128), jnp.float32),
+            pltpu.VMEM((8 * RT, 1), jnp.float32),
+            pltpu.VMEM((RT, MAXP * PT + 128), jnp.float32),
             dma((4, 8)),
             dma((4, 8)),
+            dma((3,)),
+            dma((3,)),
             dma((4,)),
             dma((4,)),
             dma((3,)),

time: 123 us -> 118 us (0.959)
  Pallas kernels: 120 us -> 115 us
    pallas_call x1, Pallas kernels: 120 us -> 115 us  [body(): pl.pallas_call(kernel, out_shape=jax.ShapeDtypeStruct((REQ_DEV * RT, GROU...]
where the time goes in v3:
time: 118 us; the launch traced here: 117 us
  Pallas kernels  115 us (97%)
  local copies, waits for them, and re-layouts  2.47 us (2%)
    pallas_call x1, Pallas kernels, body(): pl.pallas_call(kernel, out_shape=jax.ShapeDtypeStruct((REQ_DEV * RT, GROU...  115 us
    unnamed x1, local copies, waits for them, and re-layouts  2.47 us

profile of v3, /device:TPU:1, one launch (start us, length us, event | category | flops | bytes accessed | tf_op | source)
XLA Modules:
  0.0 117.3 jit_solution(555878441119807040)
XLA Ops:
  0.0 114.8 %shard_map.109 = bf16[640,1024]{1,0:T(8,128)(2,1)} custom-call(bf16[640,2048]{1,0:T(8,128)(2,1)} %hidden.1, f32[1,8192]{1,0:T(1,128)} %bitcast.5, bf16[8192,1024]{1,0:T(8,128)(2,1)} %w_query.1, bf16[8192,128]{1,0:T(8,128)(2,1)} %w_key.1, bf16[8192,128]{1,0:T(8,128)(2,1)} %w_value.1, bf16[8,256,256]{2,1,0:T(8,128)(2,1)} %bitcast.4, bf16[32,256]{1,0:T(8,128)(2,1)} %bitcast.6, ...), custom_call_target="tpu_custom_call" | custom-call | tf_op jit(solution)/shard_map/pallas_call | solution.py:555
  114.8 2.5 %copy.13 = bf16[640,1024]{1,0:T(8,128)(2,1)} copy(bf16[640,1024]{1,0:T(8,128)(2,1)} %shard_map.109) | data formatting | bytes 2621440

commit v4 on v3

--- a/solution.py
+++ b/solution.py
@@ -487,9 +487,17 @@
             for db, dc in others:
                 bs_copy(db, dc, via_index((4 - db) % 4, dc)).wait_recv()
 
-        @pl.when((t == 3) | (t == 4) | (t == 6) | (t == 7))
-        def _():
-            project_near(jnp.where(t > 4, t - 4, t - 3))
+        @pl.when(t == 6)
+        def _():
+            for db, dc in others:
+                for off in range(SIDE):
+                    b_copy(db, dc, off, via_index((4 - db) % 4, dc)).wait_recv()
+
+        @pl.when(t >= 6)
+        def _():
+            begin = jnp.where(t == 6, 0, jnp.where(t == 7, 2, 6))
+            end = jnp.where(t == 6, 2, jnp.where(t == 9, 8, 6))
+            lax.fori_loop(begin, end, own, 0)
 
         @pl.when((t == 3) | (t == 5) | (t == 6) | (t == 8))
         def _():
@@ -497,21 +505,13 @@
             project_far(k)
             lax.fori_loop(2 * k, 2 * k + 2, shared, 0)
 
-        @pl.when(t == 6)
-        def _():
-            for db, dc in others:
-                for off in range(SIDE):
-                    b_copy(db, dc, off, via_index((4 - db) % 4, dc)).wait_recv()
-
-        @pl.when(t >= 6)
-        def _():
-            begin = jnp.where(t == 6, 0, 4 * t - 26)
-            end = jnp.where(t == 6, 2, 2 * t - 8)
-            lax.fori_loop(begin, end, own, 0)
+        @pl.when((t == 2) | (t == 4) | (t == 5) | (t == 7))
+        def _():
+            project_near((t - 1) // 2)
 
         return 0
 
-    lax.fori_loop(0, 9, step, 0)
+    lax.fori_loop(0, 10, step, 0)
 
     def finish(t, _):
         for way in range(2):

time: 118 us -> 116 us (0.983)
  Pallas kernels: 115 us -> 113 us
    pallas_call x1, Pallas kernels: 115 us -> 113 us  [body(): pl.pallas_call(kernel, out_shape=jax.ShapeDtypeStruct((REQ_DEV * RT, GROU...]
where the time goes in v4:
time: 116 us; the launch traced here: 115 us
  Pallas kernels  113 us (97%)
  local copies, waits for them, and re-layouts  2.47 us (2%)
    pallas_call x1, Pallas kernels, body(): pl.pallas_call(kernel, out_shape=jax.ShapeDtypeStruct((REQ_DEV * RT, GROU...  113 us
    unnamed x1, local copies, waits for them, and re-layouts  2.47 us

profile of v4, /device:TPU:1, one launch (start us, length us, event | category | flops | bytes accessed | tf_op | source)
XLA Modules:
  0.0 115.3 jit_solution(5800886490227355952)
XLA Ops:
  0.0 112.8 %shard_map.109 = bf16[640,1024]{1,0:T(8,128)(2,1)} custom-call(bf16[640,2048]{1,0:T(8,128)(2,1)} %hidden.1, f32[1,8192]{1,0:T(1,128)} %bitcast.5, bf16[8192,1024]{1,0:T(8,128)(2,1)} %w_query.1, bf16[8192,128]{1,0:T(8,128)(2,1)} %w_key.1, bf16[8192,128]{1,0:T(8,128)(2,1)} %w_value.1, bf16[8,256,256]{2,1,0:T(8,128)(2,1)} %bitcast.4, bf16[32,256]{1,0:T(8,128)(2,1)} %bitcast.6, ...), custom_call_target="tpu_custom_call" | custom-call | tf_op jit(solution)/shard_map/pallas_call | solution.py:555
  112.9 2.5 %copy.13 = bf16[640,1024]{1,0:T(8,128)(2,1)} copy(bf16[640,1024]{1,0:T(8,128)(2,1)} %shard_map.109) | data formatting | bytes 2621440

commit v5 on v4

--- a/solution.py
+++ b/solution.py
@@ -495,8 +495,8 @@
 
         @pl.when(t >= 6)
         def _():
-            begin = jnp.where(t == 6, 0, jnp.where(t == 7, 2, 6))
-            end = jnp.where(t == 6, 2, jnp.where(t == 9, 8, 6))
+            begin = jnp.where(t == 6, 0, jnp.where(t == 7, 3, 6))
+            end = jnp.where(t == 6, 3, jnp.where(t == 9, 8, 6))
             lax.fori_loop(begin, end, own, 0)
 
         @pl.when((t == 3) | (t == 5) | (t == 6) | (t == 8))

time: 116 us -> 114 us (0.983)
    pallas_call x1, Pallas kernels: 113 us -> 112 us  [body(): pl.pallas_call(kernel, out_shape=jax.ShapeDtypeStruct((REQ_DEV * RT, GROU...]
where the time goes in v5:
time: 114 us
  Pallas kernels  112 us (98%)
  local copies, waits for them, and re-layouts  2.47 us (2%)
    pallas_call x1, Pallas kernels, body(): pl.pallas_call(kernel, out_shape=jax.ShapeDtypeStruct((REQ_DEV * RT, GROU...  112 us
    unnamed x1, local copies, waits for them, and re-layouts  2.47 us

profile of v5, /device:TPU:1, one launch (start us, length us, event | category | flops | bytes accessed | tf_op | source)
XLA Modules:
  0.0 114.1 jit_solution(4628144695399902456)
XLA Ops:
  0.0 111.7 %shard_map.109 = bf16[640,1024]{1,0:T(8,128)(2,1)} custom-call(bf16[640,2048]{1,0:T(8,128)(2,1)} %hidden.1, f32[1,8192]{1,0:T(1,128)} %bitcast.5, bf16[8192,1024]{1,0:T(8,128)(2,1)} %w_query.1, bf16[8192,128]{1,0:T(8,128)(2,1)} %w_key.1, bf16[8192,128]{1,0:T(8,128)(2,1)} %w_value.1, bf16[8,256,256]{2,1,0:T(8,128)(2,1)} %bitcast.4, bf16[32,256]{1,0:T(8,128)(2,1)} %bitcast.6, ...), custom_call_target="tpu_custom_call" | custom-call | tf_op jit(solution)/shard_map/pallas_call | solution.py:555
  111.7 2.5 %copy.13 = bf16[640,1024]{1,0:T(8,128)(2,1)} copy(bf16[640,1024]{1,0:T(8,128)(2,1)} %shard_map.109) | data formatting | bytes 2621440
